TPU v7x, 32 devices: a whole 2x2x4 slice. The times are simulated.
32 devices in a mesh: dp: 16 (over z, y, x), mp: 2 (over core).
Axes of the slice: x: 2, y: 2, z: 4, core: 2. Of those that a mesh axis runs over, the one named last changes fastest.
Arguments:
- inputs: bfloat16 [16, 1024, 1024], P('dp', 'mp'), may hold values from -6 to 6
- memory: bfloat16 [16, 384, 1024], P('dp'), may hold values from -6 to 6
- compressed_memory: bfloat16 [16, 512, 1024], P('dp'), may hold values from -6 to 6
- doc_starts: int32 [16, 4], P('dp'), may hold values from 0 to 991, as said below
- mem_valid: int32 [16], P('dp'), may hold values from 1 to 384
- cmem_valid: int32 [16], P('dp'), may hold values from 1 to 512
- gain_attn: float32 [1024], replicated, may hold values from 0.5 to 1.5
- w_qkv: bfloat16 [3, 1024, 1024], P(None, None, 'mp'), may hold values from -0.1875 to 0.1875
- slopes: float32 [8], P('mp'), may hold values from 0.00026041668 to 0.05
- w_out: bfloat16 [1024, 1024], P('mp'), may hold values from -1.5 to 1.5
- gain_ffn: float32 [1024], replicated, may hold values from 0.5 to 1.5
- w_up: bfloat16 [1024, 4096], P(None, 'mp'), may hold values from -0.1875 to 0.1875
- w_down: bfloat16 [4096, 1024], P('mp'), may hold values from -0.09375 to 0.09375
- w_comp: bfloat16 [3, 1024, 1024], P(None, None, 'mp'), may hold values from -0.109375 to 0.109375
- out_grad: bfloat16 [16, 1024, 1024], P('dp', 'mp'), may hold values from -6 to 6
- comp_grad: bfloat16 [16, 128, 1024], P('dp', None, 'mp'), may hold values from -6 to 6
Outputs:
- output: bfloat16 [16, 1024, 1024], P('dp', 'mp')
- compressed: bfloat16 [16, 128, 1024], P('dp', None, 'mp')
- input_grad: bfloat16 [16, 1024, 1024], P('dp', 'mp')
- gain_attn_grad: float32 [1024], replicated
- w_qkv_grad: float32 [3, 1024, 1024], P(None, 'dp', 'mp')
- slopes_grad: float32 [8], P('mp')
- w_out_grad: float32 [1024, 1024], P('mp', 'dp')
- gain_ffn_grad: float32 [1024], replicated
- w_up_grad: float32 [1024, 4096], P('dp', 'mp')
- w_down_grad: float32 [4096, 1024], P('mp', 'dp')
- w_comp_grad: float32 [3, 1024, 1024], P(None, 'dp', 'mp')
Inputs may be any that keep to these rules, and one draw needn't show every extreme that they name: `doc_starts`: each row begins with 0 and rises strictly; the second document of each sequence starts below 512 and the third at or above it.
All inputs are finite; a program needn't handle non-finite values.
Results may differ from a plain program's by a relative error of at most 0.014.
Values may be sent and summed in bfloat16 or wider, within the bound.
No kernel may reach another device: no remote copies, remote signals or barrier semaphores. Data moves between devices by JAX's collectives and lax.ppermute only.
A program may use at most 256 MiB of HBM per device.

v0:
```python
from functools import partial

import jax
import jax.numpy as jnp
from jax import lax
from jax.sharding import PartitionSpec as P


def normalize(rows, gain):
    centre = jnp.mean(rows, axis=-1, keepdims=True)
    centred = rows - centre
    spread = jnp.mean(centred * centred, axis=-1, keepdims=True)
    return centred * lax.rsqrt(spread + 1e-05) * gain


def gelu_exact(values_in):
    return jax.nn.gelu(values_in, approximate=False)


def visibility(query_pos, starts, mem_len, cmem_len, seq_len, mem_rows, cmem_rows):
    key_tokens = jnp.arange(seq_len, dtype=jnp.int32)
    doc_query = jnp.sum((query_pos[:, None] >= starts[None, :]).astype(jnp.int32), axis=1)
    doc_key = jnp.sum((key_tokens[:, None] >= starts[None, :]).astype(jnp.int32), axis=1)
    see_tokens = (key_tokens[None, :] <= query_pos[:, None]) & (
        doc_key[None, :] == doc_query[:, None]
    )
    first_doc = (doc_query == 1)[:, None]
    cmem_index = jnp.arange(cmem_rows, dtype=jnp.int32)
    mem_index = jnp.arange(mem_rows, dtype=jnp.int32)
    see_cmem = first_doc & (cmem_index >= cmem_rows - cmem_len)[None, :]
    see_mem = first_doc & (mem_index >= mem_rows - mem_len)[None, :]
    visible = jnp.concatenate([see_cmem, see_mem, see_tokens], axis=1)
    key_pos = jnp.concatenate(
        [-mem_rows - 3 * (cmem_rows - cmem_index), mem_index - mem_rows, key_tokens]
    )
    distance = (query_pos[:, None] - key_pos[None, :]).astype(jnp.float32)
    return (visible, distance)


def shards(
    inputs,
    memory,
    compressed_memory,
    doc_starts,
    mem_valid,
    cmem_valid,
    gain_attn,
    w_qkv,
    slopes,
    w_out,
    gain_ffn,
    w_up,
    w_down,
    w_comp,
    out_grad,
    comp_grad,
):
    x_float = inputs[0].astype(jnp.float32)
    starts = doc_starts[0]
    mem_len = mem_valid[0]
    cmem_len = cmem_valid[0]
    mem_float = memory[0].astype(jnp.float32)
    cmem_float = compressed_memory[0].astype(jnp.float32)
    mem_rows = memory.shape[1]
    cmem_rows = compressed_memory.shape[1]
    mem_total = mem_rows + cmem_rows
    width = inputs.shape[2]
    normed_local = normalize(x_float, gain_attn)
    normed = lax.all_gather(normed_local.astype(jnp.bfloat16), "mp", axis=0, tiled=True)
    seq_len = normed.shape[0]
    context = jnp.concatenate(
        [
            normalize(cmem_float, gain_attn).astype(jnp.bfloat16),
            normalize(mem_float, gain_attn).astype(jnp.bfloat16),
            normed,
        ],
        axis=0,
    )
    keys_len = context.shape[0]
    heads = slopes.shape[0]
    head_dim = w_qkv.shape[2] // heads
    scale = head_dim ** (-0.5)
    queries = (
        jnp.dot(normed, w_qkv[0], preferred_element_type=jnp.float32)
        .astype(jnp.bfloat16)
        .reshape(seq_len, heads, head_dim)
    )
    keys_all = (
        jnp.dot(context, w_qkv[1], preferred_element_type=jnp.float32)
        .astype(jnp.bfloat16)
        .reshape(keys_len, heads, head_dim)
    )
    values_all = (
        jnp.dot(context, w_qkv[2], preferred_element_type=jnp.float32)
        .astype(jnp.bfloat16)
        .reshape(keys_len, heads, head_dim)
    )
    block_rows = min(512, seq_len)
    block_starts = jnp.arange(seq_len // block_rows, dtype=jnp.int32) * block_rows

    def scores_of(start):
        query_pos = start + jnp.arange(block_rows, dtype=jnp.int32)
        visible, distance = visibility(
            query_pos, starts, mem_len, cmem_len, seq_len, mem_rows, cmem_rows
        )
        query_block = lax.dynamic_slice_in_dim(queries, start, block_rows, 0)
        raw = (
            jnp.einsum("qhd,khd->hqk", query_block, keys_all, preferred_element_type=jnp.float32)
            * scale
        )
        raw = raw - slopes[:, None, None] * distance[None]
        return (jnp.where(visible[None], raw, -1e30), query_block, distance)

    def forward_block(start):
        scores, query_block, distance = scores_of(start)
        row_max = jnp.max(scores, axis=-1, keepdims=True)
        exp_terms = jnp.exp(scores - row_max)
        row_total = jnp.sum(exp_terms, axis=-1, keepdims=True)
        weights_low = (exp_terms / row_total).astype(jnp.bfloat16)
        block_out = jnp.einsum(
            "hqk,khd->qhd", weights_low, values_all, preferred_element_type=jnp.float32
        ).astype(jnp.bfloat16)
        return (block_out, (row_max + jnp.log(row_total))[..., 0])

    attended, log_totals = lax.map(forward_block, block_starts)
    attended = attended.reshape(seq_len, heads * head_dim)
    attn_part = jnp.dot(attended, w_out, preferred_element_type=jnp.float32)
    attn_total = lax.psum_scatter(attn_part, "mp", scatter_dimension=0, tiled=True)
    middle = x_float + attn_total
    normed_ffn_local = normalize(middle, gain_ffn)
    normed_ffn = lax.all_gather(normed_ffn_local.astype(jnp.bfloat16), "mp", axis=0, tiled=True)
    pre_act = jnp.dot(normed_ffn, w_up, preferred_element_type=jnp.float32)
    hidden = gelu_exact(pre_act).astype(jnp.bfloat16)
    ffn_part = jnp.dot(hidden, w_down, preferred_element_type=jnp.float32)
    ffn_total = lax.psum_scatter(
        ffn_part.astype(jnp.bfloat16), "mp", scatter_dimension=0, tiled=True
    ).astype(jnp.float32)
    result = (middle + ffn_total).astype(jnp.bfloat16)
    mem_groups = memory[0].reshape(mem_rows // 3, 3 * width)
    compressed = jnp.dot(
        mem_groups, w_comp.reshape(3 * width, w_comp.shape[2]), preferred_element_type=jnp.float32
    ).astype(jnp.bfloat16)
    grad_rows = lax.all_gather(out_grad[0], "mp", axis=0, tiled=True)
    grad_hidden = jnp.einsum("le,fe->lf", grad_rows, w_down, preferred_element_type=jnp.float32)
    _, gelu_back = jax.vjp(gelu_exact, pre_act)
    grad_pre = gelu_back(grad_hidden)[0].astype(jnp.bfloat16)
    grad_down = jnp.einsum("lf,le->fe", hidden, grad_rows, preferred_element_type=jnp.float32)
    grad_up = jnp.einsum("ld,lf->df", normed_ffn, grad_pre, preferred_element_type=jnp.float32)
    grad_up_part, grad_down_part = (
        lax.psum_scatter(grad_up, "dp", scatter_dimension=0, tiled=True),
        lax.psum_scatter(grad_down, "dp", scatter_dimension=1, tiled=True),
    )
    grad_normed_ffn = lax.psum_scatter(
        jnp.einsum("lf,df->ld", grad_pre, w_up, preferred_element_type=jnp.float32),
        "mp",
        scatter_dimension=0,
        tiled=True,
    )
    _, ffn_norm_back = jax.vjp(normalize, middle, gain_ffn)
    grad_middle_norm, grad_gain_ffn = ffn_norm_back(grad_normed_ffn)
    grad_middle = out_grad[0].astype(jnp.float32) + grad_middle_norm
    grad_attn_rows = lax.all_gather(grad_middle.astype(jnp.bfloat16), "mp", axis=0, tiled=True)
    grad_out = jnp.einsum("lh,le->he", attended, grad_attn_rows, preferred_element_type=jnp.float32)
    grad_attended = (
        jnp.einsum("le,he->lh", grad_attn_rows, w_out, preferred_element_type=jnp.float32)
        .astype(jnp.bfloat16)
        .reshape(seq_len, heads, head_dim)
    )

    def backward_block(carry, block_item):
        grad_keys, grad_values, grad_slopes = carry
        start, block_log_total = block_item
        scores, query_block, distance = scores_of(start)
        weights_full = jnp.exp(scores - block_log_total[..., None])
        grad_block = lax.dynamic_slice_in_dim(grad_attended, start, block_rows, 0)
        grad_weights = jnp.einsum(
            "qhd,khd->hqk", grad_block, values_all, preferred_element_type=jnp.float32
        )
        row_inner = jnp.sum(weights_full * grad_weights, axis=-1, keepdims=True)
        grad_scores = (weights_full * (grad_weights - row_inner)).astype(jnp.bfloat16)
        grad_slopes = grad_slopes - jnp.sum(
            grad_scores.astype(jnp.float32) * distance[None], axis=(1, 2)
        )
        grad_query = (
            jnp.einsum("hqk,khd->qhd", grad_scores, keys_all, preferred_element_type=jnp.float32)
            * scale
        )
        grad_keys = (
            grad_keys
            + jnp.einsum(
                "hqk,qhd->khd", grad_scores, query_block, preferred_element_type=jnp.float32
            )
            * scale
        )
        grad_values = grad_values + jnp.einsum(
            "hqk,qhd->khd",
            weights_full.astype(jnp.bfloat16),
            grad_block,
            preferred_element_type=jnp.float32,
        )
        return ((grad_keys, grad_values, grad_slopes), grad_query.astype(jnp.bfloat16))

    zero_keys = jnp.zeros((keys_len, heads, head_dim), jnp.float32)
    carried, grad_queries = lax.scan(
        backward_block,
        (zero_keys, zero_keys, jnp.zeros((heads,), jnp.float32)),
        (block_starts, log_totals),
    )
    grad_keys_low = carried[0].astype(jnp.bfloat16).reshape(keys_len, heads * head_dim)
    grad_values_low = carried[1].astype(jnp.bfloat16).reshape(keys_len, heads * head_dim)
    grad_slopes = carried[2]
    grad_queries = grad_queries.reshape(seq_len, heads * head_dim)
    grad_qkv = jnp.stack(
        [
            jnp.einsum("ld,lh->dh", normed, grad_queries, preferred_element_type=jnp.float32),
            jnp.einsum("ld,lh->dh", context, grad_keys_low, preferred_element_type=jnp.float32),
            jnp.einsum("ld,lh->dh", context, grad_values_low, preferred_element_type=jnp.float32),
        ]
    )
    grad_context = jnp.einsum(
        "lh,dh->ld", grad_keys_low, w_qkv[1], preferred_element_type=jnp.float32
    ) + jnp.einsum("lh,dh->ld", grad_values_low, w_qkv[2], preferred_element_type=jnp.float32)
    grad_normed_part = (
        jnp.einsum("lh,dh->ld", grad_queries, w_qkv[0], preferred_element_type=jnp.float32)
        + grad_context[mem_total:]
    )
    grad_normed = lax.psum_scatter(
        grad_normed_part.astype(jnp.bfloat16), "mp", scatter_dimension=0, tiled=True
    ).astype(jnp.float32)
    _, attn_norm_back = jax.vjp(normalize, x_float, gain_attn)
    grad_x_norm, grad_gain_tokens = attn_norm_back(grad_normed)
    grad_inputs = (grad_middle + grad_x_norm).astype(jnp.bfloat16)
    _, cmem_norm_back = jax.vjp(partial(normalize, cmem_float), gain_attn)
    _, mem_norm_back = jax.vjp(partial(normalize, mem_float), gain_attn)
    grad_gain_attn = (
        grad_gain_tokens
        + cmem_norm_back(grad_context[:cmem_rows])[0]
        + mem_norm_back(grad_context[cmem_rows:mem_total])[0]
    )
    grad_comp = jnp.einsum(
        "ir,id->rd", mem_groups, comp_grad[0], preferred_element_type=jnp.float32
    ).reshape(3, width, w_comp.shape[2])
    grad_qkv_part, grad_out_part, grad_comp_part = (
        lax.psum_scatter(grad_qkv, "dp", scatter_dimension=1, tiled=True),
        lax.psum_scatter(grad_out, "dp", scatter_dimension=1, tiled=True),
        lax.psum_scatter(grad_comp, "dp", scatter_dimension=1, tiled=True),
    )
    slopes_total = lax.psum(grad_slopes, "dp")
    gain_attn_total, gain_ffn_total = lax.psum((grad_gain_attn, grad_gain_ffn), ("dp", "mp"))
    return (
        result[None],
        compressed[None],
        grad_inputs[None],
        gain_attn_total,
        grad_qkv_part,
        slopes_total,
        grad_out_part,
        gain_ffn_total,
        grad_up_part,
        grad_down_part,
        grad_comp_part,
    )


def solution(mesh):
    placed = (
        P("dp", "mp", None),
        P("dp", None, None),
        P("dp", None, None),
        P("dp", None),
        P("dp"),
        P("dp"),
        P(),
        P(None, None, "mp"),
        P("mp"),
        P("mp", None),
        P(),
        P(None, "mp"),
        P("mp", None),
        P(None, None, "mp"),
        P("dp", "mp", None),
        P("dp", None, "mp"),
    )
    return jax.shard_map(
        shards,
        mesh=mesh,
        in_specs=placed,
        out_specs=(
            P("dp", "mp", None),
            P("dp", None, "mp"),
            P("dp", "mp", None),
            P(),
            P(None, "dp", "mp"),
            P("mp"),
            P("mp", "dp"),
            P(),
            P("dp", "mp"),
            P("mp", "dp"),
            P(None, "dp", "mp"),
        ),
        check_vma=False,
    )
```

profile of v0, /device:TPU:0, one launch (start us, length us, event | category | flops | bytes accessed | tf_op | source)
XLA Modules:
  0.0 1155.0 jit_solution(8199716677788884228)
XLA Ops:
  57.7 66.7 %while.33 = (s32[]{:T(128)}, bf16[2,512,4,128]{3,2,1,0:T(4,128)(2,1)}, f32[2,4,512]{2,1,0:T(4,128)S(1)}, s32[2]{0:T(128)S(1)}, s32[1,4]{1,0:T(1,128)S(1)}, /*ind...) while((s32[]{:T(128)}, ...), condition=%wide.region_11.12_spmd, body=%wide.region_6.11_spmd.sunk | while | flops 2090293248 | bytes 103276696 | solution.py:125
  71.0 8.7 fusion.160
  79.7 10.1 fusion.161
  112.9 10.1 fusion.161
  129.3 13.3 %reduce-scatter.10.cloned.1.call-done = f32[512,1024]{1,0:T(8,128)} async-done(((f32[1024,1024]{1,0:T(8,128)}), f32[512,1024]{1,0:T(8,128)}) %reduce-scatter.10.cloned.1.call-update) | async-done | bytes 2097168 | tf_op jit(solution)/shard_map/reduce_scatter | solution.py:128
  148.0 11.4 all-gather.8.cloned.1.call-done
  159.4 37.4 %multiply_convert_fusion.1 = (bf16[1024,2048]{1,0:T(8,128)(2,1)}, f32[1024,2048]{1,0:T(8,128)}, f32[1024,2048]{1,0:T(8,128)}) fusion(bf16[1024,1024]{1,0:T(8,128)(2,1)} %all-gather.8.cloned.1.call-done, bf16[1024,2048]{1,0:T(8,128)(2,1)} %param.31), kind=kOutput, calls=%fused_computation.74 | convolution fusion | flops 4431282176 | bytes 27262976 | tf_op jit(solution)/shard_map/dot_general | solution.py:132
  196.8 12.8 %add_convert_fusion = bf16[1024,2048]{1,0:T(8,128)(2,1)S(1)} fusion(f32[1024,2048]{1,0:T(8,128)} %get-tuple-element.540, f32[1024,2048]{1,0:T(8,128)} %get-tuple-element.554, bf16[2048,1024]{1,0:T(8,128)(2,1)} %param.32, bf16[1,1024,1024]{2,1,0:T(8,128)(2,1)} %all-gather.12.cloned.1.call-done), kind=kOutput, calls=%fused_computation.73 | convolution fusion | flops 4324327424 | bytes 27262976 | tf_op jit(solution)/shard_map/le,fe->lf/dot_general | solution.py:144
  217.9 9.2 convolution_convert_fusion.2
  234.7 9.5 reduce-scatter.12.cloned.1.call-done
  251.3 11.8 %all-gather.10.cloned.1.call-done = bf16[1024,1024]{1,0:T(8,128)(2,1)} async-done(((bf16[512,1024]{1,0:T(8,128)(2,1)}), bf16[1024,1024]{1,0:T(8,128)(2,1)}) %all-gather.10.cloned.1.call-update) | async-done | bytes 2097168 | tf_op jit(solution)/shard_map/all_gather | solution.py:162
  268.5 122.3 %while.34 = (s32[]{:T(128)}, f32[1920,4,128]{0,2,1:T(8,128)}, f32[1920,4,128]{0,2,1:T(8,128)}, f32[4]{0:T(128)S(1)}, bf16[2,512,4,128]{3,2,1,0:T(4,128)(2,1)}, /...) while((s32[]{:T(128)}, f32[1920,4,128]{0,2,1:T(8,128)}, ...), condition=%wide.region_24.25_spmd.clone, body=%wide.region_19.0_spmd.clone.sunk | while | flops 5099640832 | bytes 321617856 | solution.py:204
  281.7 14.0 %multiply_reduce_fusion.7 = (f32[4,512]{1,0:T(4,128)S(1)}, f32[4,512,1920]{2,1,0:T(8,128)}) fusion(f32[4,512,1920]{2,1,0:T(8,128)} %fusion.171, f32[4,512]{1,0:T(4,128)S(1)} %dynamic-slice_bitcast_fusion.2, f32[512,1920]{1,0:T(8,128)S(1)} %subtract_convert_fusion.5, f32[4]{0:T(128)S(1)} %get-tuple-element.822, ...), kind=kOutput, calls=%fused_computation.33.clone.1 | convolution fusion | flops 1034156032 | bytes 38879252 | tf_op jit(solution)/shard_map/while/body/eval_jaxpr/qhd,khd->hqk/dot_general | solution.py:108
  295.7 15.0 %multiply_reduce_fusion.8 = (f32[4]{0:T(128)S(1)}, bf16[4,512,1920]{2,1,0:T(8,128)(2,1)}) fusion(f32[512,1920]{1,0:T(8,128)S(1)} %subtract_convert_fusion.5, f32[4,512,1920]{2,1,0:T(8,128)} %get-tuple-element.729, f32[4,512,1920]{2,1,0:T(8,128)} %fusion.171, f32[4,512]{1,0:T(4,128)S(1)} %get-tuple-element.730), kind=kLoop, calls=%fused_computation.31.clone.1 | loop fusion | flops 23592956 | bytes 43261968 | tf_op jit(solution)/shard_map/while/body/eval_jaxpr/reduce_sum | solution.py:181
  341.5 14.0 %multiply_reduce_fusion.7 = (f32[4,512]{1,0:T(4,128)S(1)}, f32[4,512,1920]{2,1,0:T(8,128)}) fusion(f32[4,512,1920]{2,1,0:T(8,128)} %fusion.171, f32[4,512]{1,0:T(4,128)S(1)} %dynamic-slice_bitcast_fusion.2, f32[512,1920]{1,0:T(8,128)S(1)} %subtract_convert_fusion.5, f32[4]{0:T(128)S(1)} %get-tuple-element.822, ...), kind=kOutput, calls=%fused_computation.33.clone.1 | convolution fusion | flops 1034156032 | bytes 38879252 | tf_op jit(solution)/shard_map/while/body/eval_jaxpr/qhd,khd->hqk/dot_general | solution.py:108
  355.5 15.0 %multiply_reduce_fusion.8 = (f32[4]{0:T(128)S(1)}, bf16[4,512,1920]{2,1,0:T(8,128)(2,1)}) fusion(f32[512,1920]{1,0:T(8,128)S(1)} %subtract_convert_fusion.5, f32[4,512,1920]{2,1,0:T(8,128)} %get-tuple-element.729, f32[4,512,1920]{2,1,0:T(8,128)} %fusion.171, f32[4,512]{1,0:T(4,128)S(1)} %get-tuple-element.730), kind=kLoop, calls=%fused_computation.31.clone.1 | loop fusion | flops 23592956 | bytes 43261968 | tf_op jit(solution)/shard_map/while/body/eval_jaxpr/reduce_sum | solution.py:181
  421.6 10.7 fusion.55
  432.3 10.6 fusion.106
  457.6 42.8 %psum.22 = f32[4]{0:T(128)} all-reduce(f32[4]{0:T(128)S(1)} %get-tuple-element.350), channel_id=1, replica_groups=mesh['dp'=16,'mp'=2] {'dp'}, use_global_device_ids=true, to_apply=%region_33.34 | all-reduce | flops 4 | bytes 32 | tf_op jit(solution)/shard_map/psum | solution.py:248
  509.9 39.6 %all-reduce = (f32[1024]{0:T(1024)}, f32[1024]{0:T(1024)}) all-reduce(f32[1024]{0:T(1024)S(1)} %add_add_fusion.2, f32[1024]{0:T(1024)S(1)} %copy-done.55), channel_id=1, replica_groups=mesh['dp'=16,'mp'=2] {'dp','mp'}, use_global_device_ids=true, to_apply=%region_31.32 | all-reduce | flops 2048 | bytes 16384 | tf_op jit(solution)/shard_map/psum | solution.py:249
  561.1 84.3 %reduce-scatter.20.cloned.1.call-done = f32[512,64]{0,1:T(8,128)} async-done(((f32[512,1024]{0,1:T(8,128)}), f32[512,64]{0,1:T(8,128)}) %reduce-scatter.20.cloned.1.call-update) | async-done | bytes 131088 | tf_op jit(solution)/shard_map/reduce_scatter | solution.py:245
  645.5 178.1 %reduce-scatter.24.cloned.1.call-done = f32[2048,64]{0,1:T(8,128)} async-done(((f32[2048,1024]{0,1:T(8,128)}), f32[2048,64]{0,1:T(8,128)}) %reduce-scatter.24.cloned.1.call-update) | async-done | bytes 524304 | tf_op jit(solution)/shard_map/reduce_scatter | solution.py:151
  823.6 183.0 %reduce-scatter.22.cloned.1.call-done = f32[64,2048]{1,0:T(8,128)} async-done(((f32[1024,2048]{1,0:T(8,128)}), f32[64,2048]{1,0:T(8,128)}) %reduce-scatter.22.cloned.1.call-update) | async-done | bytes 524304 | tf_op jit(solution)/shard_map/reduce_scatter | solution.py:150
  1006.6 141.5 %reduce-scatter.18.cloned.1.call-done = f32[3,64,512]{2,1,0:T(8,128)} async-done(((f32[3,1024,512]{2,1,0:T(8,128)}), f32[3,64,512]{2,1,0:T(8,128)}) %reduce-scatter.18.cloned.1.call-update) | async-done | bytes 393232 | tf_op jit(solution)/shard_map/reduce_scatter | solution.py:244
  (324 shorter events, 246.5 us)
Async XLA Ops:
  7.2 448.0 %copy-start = (bf16[3,1024,512]{2,1,0:T(8,128)(2,1)S(1)}, bf16[3,1024,512]{2,1,0:T(8,128)(2,1)}, u32[]{:S(2)}) copy-start(bf16[3,1024,512]{2,1,0:T(8,128)(2,1)} %param.33) | copy-start | bytes 9437188
  7.2 22.6 %all-gather.6.cloned.1.call-start = ((), (), s32[]{:S(2)}) async-start(), calls=%async_computation.9 | async-start | bytes 3145728 | tf_op jit(solution)/shard_map/all_gather | solution.py:69
  16.4 126.2 %reduce-scatter.10.cloned.1.call-start = ((), (), s32[]{:S(2)}) async-start(), calls=%async_computation.10 | async-start | bytes 6291456 | tf_op jit(solution)/shard_map/reduce_scatter | solution.py:128
  129.2 30.2 %all-gather.8.cloned.1.call-start = ((), (), s32[]{:S(2)}) async-start(), calls=%async_computation.11 | async-start | bytes 3145728 | tf_op jit(solution)/shard_map/all_gather | solution.py:131
  147.4 49.4 %all-gather.12.cloned.1.call-start = ((), (), s32[]{:S(2)}) async-start(), calls=%async_computation.21 | async-start | bytes 3145728 | tf_op jit(solution)/shard_map/all_gather | solution.py:143
  148.0 83.2 %reduce-scatter.14.cloned.1.call-start = ((), (), s32[]{:S(2)}) async-start(), calls=%async_computation.13 | async-start | bytes 6291456 | tf_op jit(solution)/shard_map/reduce_scatter | solution.py:153
  217.8 26.4 %reduce-scatter.12.cloned.1.call-start = ((), (), s32[]{:S(2)}) async-start(), calls=%async_computation.12 | async-start | bytes 3145728 | tf_op jit(solution)/shard_map/reduce_scatter | solution.py:135
  227.2 36.0 %all-gather.10.cloned.1.call-start = ((), (), s32[]{:S(2)}) async-start(), calls=%async_computation.14 | async-start | bytes 3145728 | tf_op jit(solution)/shard_map/all_gather | solution.py:162
  251.2 253.7 %reduce-scatter.16.cloned.1.call-start = ((), (), s32[]{:S(2)}) async-start(), calls=%async_computation.15 | async-start | bytes 3145728 | tf_op jit(solution)/shard_map/reduce_scatter | solution.py:227
  295.7 17.6 %copy-start.16 = (bf16[1024,4,128]{0,2,1:T(8,128)(2,1)S(1)}, bf16[1024,4,128]{0,2,1:T(8,128)(2,1)}, u32[]{:S(2)}) copy-start(bf16[1024,4,128]{0,2,1:T(8,128)(2,1)} %get-tuple-element.824) | copy-start | bytes 3145732 | tf_op jit(solution)/shard_map/while
  407.2 154.0 %reduce-scatter.26.cloned.1.call-start = ((), (), s32[]{:S(2)}) async-start(), calls=%async_computation.20 | async-start | bytes 6684672 | tf_op jit(solution)/shard_map/reduce_scatter | solution.py:246
  416.5 229.0 %reduce-scatter.20.cloned.1.call-start = ((), (), s32[]{:S(2)}) async-start(), calls=%async_computation.17 | async-start | bytes 2228224 | tf_op jit(solution)/shard_map/reduce_scatter | solution.py:245
  421.3 402.2 %reduce-scatter.24.cloned.1.call-start = ((), (), s32[]{:S(2)}) async-start(), calls=%async_computation.19 | async-start | bytes 8912896 | tf_op jit(solution)/shard_map/reduce_scatter | solution.py:151
  432.3 574.3 %reduce-scatter.22.cloned.1.call-start = ((), (), s32[]{:S(2)}) async-start(), calls=%async_computation.18 | async-start | bytes 8912896 | tf_op jit(solution)/shard_map/reduce_scatter | solution.py:150
  443.0 705.1 %reduce-scatter.18.cloned.1.call-start = ((), (), s32[]{:S(2)}) async-start(), calls=%async_computation.16 | async-start | bytes 6684672 | tf_op jit(solution)/shard_map/reduce_scatter | solution.py:244
  455.1 45.3 %copy-start.46 = (f32[384]{0:T(512)S(1)}, f32[384]{0:T(512)}, u32[]{:S(2)}) copy-start(f32[384]{0:T(512)} %copy-done.45) | copy-start | bytes 4612
  455.1 45.3 %copy-start.52 = (f32[384]{0:T(512)S(1)}, f32[384]{0:T(512)}, u32[]{:S(2)}) copy-start(f32[384]{0:T(512)} %copy-done.51) | copy-start | bytes 4612
  455.2 47.3 %copy-start.44 = (f32[512]{0:T(512)S(1)}, f32[512]{0:T(512)}, u32[]{:S(2)}) copy-start(f32[512]{0:T(512)} %copy-done.43) | copy-start | bytes 6148
  455.2 47.3 %copy-start.48 = (f32[512]{0:T(512)S(1)}, f32[512]{0:T(512)}, u32[]{:S(2)}) copy-start(f32[512]{0:T(512)} %copy-done.47) | copy-start | bytes 6148
  455.2 49.7 %copy-start.35 = (f32[1024]{0:T(1024)S(1)}, f32[1024]{0:T(1024)}, u32[]{:S(2)}) copy-start(f32[1024]{0:T(1024)} %param.26) | copy-start | bytes 12292
  455.2 49.7 %copy-start.37 = (f32[512]{0:T(512)S(1)}, f32[512]{0:T(512)}, u32[]{:S(2)}) copy-start(f32[512]{0:T(512)} %copy-done.36) | copy-start | bytes 6148
  457.6 49.4 %copy-start.54 = (f32[512]{0:T(512)S(1)}, f32[512]{0:T(512)}, u32[]{:S(2)}) copy-start(f32[512]{0:T(512)} %copy-done.53) | copy-start | bytes 6148
  457.6 49.5 %copy-start.42 = (f32[512]{0:T(512)S(1)}, f32[512]{0:T(512)}, u32[]{:S(2)}) copy-start(f32[512]{0:T(512)} %copy-done.41) | copy-start | bytes 6148
  502.5 47.0 %copy-start.50 = (f32[512]{0:T(512)S(1)}, f32[512]{0:T(512)}, u32[]{:S(2)}) copy-start(f32[512]{0:T(512)} %copy-done.49) | copy-start | bytes 6148
  (64 other events, 370.4 us)
Sparse Core Ops, SparseCore 0:
  16.5 13.2 all-gather.5
  129.4 13.2 reduce-scatter.9
  147.5 11.8 all-gather.7
  160.9 11.7 all-gather.11
  218.0 13.1 reduce-scatter.13
  233.3 10.8 reduce-scatter.11
  251.3 11.7 all-gather.9
  407.3 10.7 reduce-scatter.15
  421.0 140.1 reduce-scatter.25
  563.8 81.5 reduce-scatter.19
  648.4 175.1 reduce-scatter.23
  826.3 180.2 reduce-scatter.21
  1009.5 138.5 reduce-scatter.17
where the time goes:
time: 1160 us
  waiting for transfers between devices  652 us (56%)
  matrix products  245 us (21%)
  other arithmetic  102 us (9%)
  blocking collectives  82.5 us (7%)
  local copies, waits for them, and re-layouts  47 us (4%)
  between operations  16.2 us (1%)
    reduce_scatter x1, waiting for transfers between devices, shards(): lax.psum_scatter(grad_up, 'dp', scatter_dimension=0, tiled=True)  183 us
    reduce_scatter x1, waiting for transfers between devices, shards(): lax.psum_scatter(grad_down, 'dp', scatter_dimension=1, tiled=True)  178 us
    reduce_scatter x1, waiting for transfers between devices, shards(): lax.psum_scatter(grad_qkv, 'dp', scatter_dimension=1, tiled=True)  141 us
    reduce_scatter x1, waiting for transfers between devices, shards(): lax.psum_scatter(grad_out, 'dp', scatter_dimension=1, tiled=True)  84.3 us
    dot_general x4, matrix products, scores_of(): jnp.einsum('qhd,khd->hqk', query_block, keys_all, preferred_element_type=...  44.1 us
    psum x1, blocking collectives, shards(): slopes_total = lax.psum(grad_slopes, 'dp')  42.8 us
    psum x1, blocking collectives, shards(): lax.psum((grad_gain_attn, grad_gain_ffn), ('dp', 'mp'))  39.6 us
    dot_general x1, matrix products, shards(): pre_act = jnp.dot(normed_ffn, w_up, preferred_element_type=jnp.float32)  37.4 us
  transfers between devices with their start and end apart: 13, of which 11 were waited for; matrix products, arithmetic and copies ran while one was open for 10% of the time, Pallas kernels for 0%

commit v1 on v0

--- a/solution.py
+++ b/solution.py
@@ -35,6 +35,58 @@
     )
     distance = (query_pos[:, None] - key_pos[None, :]).astype(jnp.float32)
     return (visible, distance)
+
+
+def swap_mp(rows):
+    return lax.ppermute(rows, "mp", [(0, 1), (1, 0)])
+
+
+def gather_mp(rows):
+    other = swap_mp(rows)
+    full = jnp.concatenate([rows, other], axis=0)
+    return jnp.roll(full, lax.axis_index("mp") * rows.shape[0], axis=0)
+
+
+def scatter_mp(rows):
+    half = rows.shape[0] // 2
+    me = lax.axis_index("mp")
+    send = lax.dynamic_slice_in_dim(rows, (1 - me) * half, half, 0)
+    keep = lax.dynamic_slice_in_dim(rows, me * half, half, 0)
+    got = swap_mp(send.astype(jnp.bfloat16))
+    return keep.astype(jnp.float32) + got.astype(jnp.float32)
+
+
+def scatter_dp(blocks, order):
+    n = lax.axis_size("dp")
+    bits = n.bit_length() - 1
+    me = lax.axis_index("dp")
+    rows, cols = blocks.shape
+    x = blocks.astype(jnp.bfloat16).reshape((2,) * bits + (rows // n, cols))
+    left = list(range(bits - 1, -1, -1))
+    for step, bit in enumerate(order):
+        axis = left.index(bit)
+        left.remove(bit)
+        mine = (me >> bit) & 1
+        send = lax.dynamic_index_in_dim(x, 1 - mine, axis, keepdims=False)
+        keep = lax.dynamic_index_in_dim(x, mine, axis, keepdims=False)
+        got = lax.ppermute(send, "dp", [(i, i ^ (1 << bit)) for i in range(n)])
+        x = keep.astype(jnp.float32) + got.astype(jnp.float32)
+        if step < bits - 1:
+            x = x.astype(jnp.bfloat16)
+    return x.reshape(rows // n, cols)
+
+
+def sum_all(vector, axes):
+    for axis in axes:
+        n = lax.axis_size(axis)
+        for bit in range(n.bit_length() - 1):
+            vector = vector + lax.ppermute(vector, axis, [(i, i ^ (1 << bit)) for i in range(n)])
+    return vector
+
+
+def order_from(first):
+    bits = lax.axis_size("dp").bit_length() - 1
+    return [(first + k) % bits for k in range(bits)]
 
 
 def shards(
@@ -66,7 +118,7 @@
     mem_total = mem_rows + cmem_rows
     width = inputs.shape[2]
     normed_local = normalize(x_float, gain_attn)
-    normed = lax.all_gather(normed_local.astype(jnp.bfloat16), "mp", axis=0, tiled=True)
+    normed = gather_mp(normed_local.astype(jnp.bfloat16))
     seq_len = normed.shape[0]
     context = jnp.concatenate(
         [
@@ -125,42 +177,37 @@
     attended, log_totals = lax.map(forward_block, block_starts)
     attended = attended.reshape(seq_len, heads * head_dim)
     attn_part = jnp.dot(attended, w_out, preferred_element_type=jnp.float32)
-    attn_total = lax.psum_scatter(attn_part, "mp", scatter_dimension=0, tiled=True)
+    attn_total = scatter_mp(attn_part)
     middle = x_float + attn_total
     normed_ffn_local = normalize(middle, gain_ffn)
-    normed_ffn = lax.all_gather(normed_ffn_local.astype(jnp.bfloat16), "mp", axis=0, tiled=True)
+    normed_ffn = gather_mp(normed_ffn_local.astype(jnp.bfloat16))
     pre_act = jnp.dot(normed_ffn, w_up, preferred_element_type=jnp.float32)
     hidden = gelu_exact(pre_act).astype(jnp.bfloat16)
     ffn_part = jnp.dot(hidden, w_down, preferred_element_type=jnp.float32)
-    ffn_total = lax.psum_scatter(
-        ffn_part.astype(jnp.bfloat16), "mp", scatter_dimension=0, tiled=True
-    ).astype(jnp.float32)
+    ffn_total = scatter_mp(ffn_part)
     result = (middle + ffn_total).astype(jnp.bfloat16)
     mem_groups = memory[0].reshape(mem_rows // 3, 3 * width)
     compressed = jnp.dot(
         mem_groups, w_comp.reshape(3 * width, w_comp.shape[2]), preferred_element_type=jnp.float32
     ).astype(jnp.bfloat16)
-    grad_rows = lax.all_gather(out_grad[0], "mp", axis=0, tiled=True)
+    grad_rows = gather_mp(out_grad[0])
     grad_hidden = jnp.einsum("le,fe->lf", grad_rows, w_down, preferred_element_type=jnp.float32)
     _, gelu_back = jax.vjp(gelu_exact, pre_act)
     grad_pre = gelu_back(grad_hidden)[0].astype(jnp.bfloat16)
-    grad_down = jnp.einsum("lf,le->fe", hidden, grad_rows, preferred_element_type=jnp.float32)
+    grad_down = jnp.einsum("lf,le->ef", hidden, grad_rows, preferred_element_type=jnp.float32)
     grad_up = jnp.einsum("ld,lf->df", normed_ffn, grad_pre, preferred_element_type=jnp.float32)
     grad_up_part, grad_down_part = (
-        lax.psum_scatter(grad_up, "dp", scatter_dimension=0, tiled=True),
-        lax.psum_scatter(grad_down, "dp", scatter_dimension=1, tiled=True),
-    )
-    grad_normed_ffn = lax.psum_scatter(
-        jnp.einsum("lf,df->ld", grad_pre, w_up, preferred_element_type=jnp.float32),
-        "mp",
-        scatter_dimension=0,
-        tiled=True,
+        scatter_dp(grad_up, order_from(0)),
+        scatter_dp(grad_down, order_from(1)).T,
+    )
+    grad_normed_ffn = scatter_mp(
+        jnp.einsum("lf,df->ld", grad_pre, w_up, preferred_element_type=jnp.float32)
     )
     _, ffn_norm_back = jax.vjp(normalize, middle, gain_ffn)
     grad_middle_norm, grad_gain_ffn = ffn_norm_back(grad_normed_ffn)
     grad_middle = out_grad[0].astype(jnp.float32) + grad_middle_norm
-    grad_attn_rows = lax.all_gather(grad_middle.astype(jnp.bfloat16), "mp", axis=0, tiled=True)
-    grad_out = jnp.einsum("lh,le->he", attended, grad_attn_rows, preferred_element_type=jnp.float32)
+    grad_attn_rows = gather_mp(grad_middle.astype(jnp.bfloat16))
+    grad_out = jnp.einsum("lh,le->eh", attended, grad_attn_rows, preferred_element_type=jnp.float32)
     grad_attended = (
         jnp.einsum("le,he->lh", grad_attn_rows, w_out, preferred_element_type=jnp.float32)
         .astype(jnp.bfloat16)
@@ -210,13 +257,11 @@
     grad_values_low = carried[1].astype(jnp.bfloat16).reshape(keys_len, heads * head_dim)
     grad_slopes = carried[2]
     grad_queries = grad_queries.reshape(seq_len, heads * head_dim)
-    grad_qkv = jnp.stack(
-        [
+    grad_qkv = (
             jnp.einsum("ld,lh->dh", normed, grad_queries, preferred_element_type=jnp.float32),
             jnp.einsum("ld,lh->dh", context, grad_keys_low, preferred_element_type=jnp.float32),
             jnp.einsum("ld,lh->dh", context, grad_values_low, preferred_element_type=jnp.float32),
-        ]
-    )
+        )
     grad_context = jnp.einsum(
         "lh,dh->ld", grad_keys_low, w_qkv[1], preferred_element_type=jnp.float32
     ) + jnp.einsum("lh,dh->ld", grad_values_low, w_qkv[2], preferred_element_type=jnp.float32)
@@ -224,9 +269,7 @@
         jnp.einsum("lh,dh->ld", grad_queries, w_qkv[0], preferred_element_type=jnp.float32)
         + grad_context[mem_total:]
     )
-    grad_normed = lax.psum_scatter(
-        grad_normed_part.astype(jnp.bfloat16), "mp", scatter_dimension=0, tiled=True
-    ).astype(jnp.float32)
+    grad_normed = scatter_mp(grad_normed_part)
     _, attn_norm_back = jax.vjp(normalize, x_float, gain_attn)
     grad_x_norm, grad_gain_tokens = attn_norm_back(grad_normed)
     grad_inputs = (grad_middle + grad_x_norm).astype(jnp.bfloat16)
@@ -237,16 +280,20 @@
         + cmem_norm_back(grad_context[:cmem_rows])[0]
         + mem_norm_back(grad_context[cmem_rows:mem_total])[0]
     )
-    grad_comp = jnp.einsum(
-        "ir,id->rd", mem_groups, comp_grad[0], preferred_element_type=jnp.float32
-    ).reshape(3, width, w_comp.shape[2])
-    grad_qkv_part, grad_out_part, grad_comp_part = (
-        lax.psum_scatter(grad_qkv, "dp", scatter_dimension=1, tiled=True),
-        lax.psum_scatter(grad_out, "dp", scatter_dimension=1, tiled=True),
-        lax.psum_scatter(grad_comp, "dp", scatter_dimension=1, tiled=True),
-    )
-    slopes_total = lax.psum(grad_slopes, "dp")
-    gain_attn_total, gain_ffn_total = lax.psum((grad_gain_attn, grad_gain_ffn), ("dp", "mp"))
+    groups = mem_groups.reshape(mem_rows // 3, 3, width)
+    grad_comp = [
+        jnp.einsum("id,ie->de", groups[:, r], comp_grad[0], preferred_element_type=jnp.float32)
+        for r in range(3)
+    ]
+    grad_comp_part = jnp.stack(
+        [scatter_dp(part, order_from(r)) for r, part in enumerate(grad_comp)]
+    )
+    grad_qkv_part = jnp.stack([scatter_dp(part, order_from(r)) for r, part in enumerate(grad_qkv)])
+    grad_out_part = scatter_dp(grad_out, order_from(2)).T
+    slopes_total = sum_all(grad_slopes, ("dp",))
+    gain_attn_total, gain_ffn_total = sum_all(
+        jnp.stack([grad_gain_attn, grad_gain_ffn]), ("mp", "dp")
+    )
     return (
         result[None],
         compressed[None],

time: 1160 us -> 611 us (0.53)
  waiting for transfers between devices: 652 us -> 126 us
  blocking collectives: 82.5 us -> 0 us
  starting transfers between devices: 1 us -> 54.6 us
  matrix products: 245 us -> 209 us
  other arithmetic: 102 us -> 128 us
  local copies, waits for them, and re-layouts: 47 us -> 72.9 us
  between operations: 16.2 us -> 3.98 us
    reduce_scatter x9 -> x0, waiting for transfers between devices: 622 us -> none  [the longest x1 183 us: shards(): lax.psum_scatter(grad_up, 'dp', scatter_dimension=0, tiled=True)]
    ppermute x0 -> x53, waiting for transfers between devices: none -> 126 us  [the longest x36 93 us: scatter_dp(): got = lax.ppermute(send, 'dp', [(i, i ^ 1 << bit) for i in range(n)])]
    psum x2 -> x0, blocking collectives: 82.5 us -> none  [the longest x1 42.8 us: shards(): slopes_total = lax.psum(grad_slopes, 'dp')]
    ppermute x0 -> x53, starting transfers between devices: none -> 54.6 us  [the longest x36 42.4 us: scatter_dp(): got = lax.ppermute(send, 'dp', [(i, i ^ 1 << bit) for i in range(n)])]
    dot_general x1, matrix products: 37.4 us -> 4.57 us  [shards(): pre_act = jnp.dot(normed_ffn, w_up, preferred_element_type=jnp.float32)]
    all_gather x4 -> x0, waiting for transfers between devices: 30.1 us -> none  [the longest x1 11.8 us: shards(): lax.all_gather(grad_middle.astype(jnp.bfloat16), 'mp', axis=0, tiled=True)]
    convert_element_type x2 -> x30, other arithmetic: 2.58 us -> 30.2 us  [the longest x27 18.3 us: scatter_dp(): x = x.astype(jnp.bfloat16)]
    dynamic_slice x0 -> x18, local copies, waits for them, and re-layouts: none -> 14.9 us  [the longest x9 9.05 us: scatter_dp(): keep = lax.dynamic_index_in_dim(x, mine, axis, keepdims=False)]
  transfers between devices with their start and end apart: 13 -> 53, of which waited for: 11 -> 23; matrix products, arithmetic and copies ran while one was open for 10% -> 54% of each run, Pallas kernels for 0% -> 0%
where the time goes in v1:
time: 611 us; the launch traced here: 603 us
  matrix products  209 us (34%)
  other arithmetic  128 us (21%)
  waiting for transfers between devices  126 us (21%)
  local copies, waits for them, and re-layouts  72.9 us (12%)
  starting transfers between devices  54.6 us (9%)
  loops' own time  9.1 us (1%)
    ppermute x36, waiting for transfers between devices, scatter_dp(): got = lax.ppermute(send, 'dp', [(i, i ^ 1 << bit) for i in range(n)])  93 us
    dot_general x4, matrix products, scores_of(): jnp.einsum('qhd,khd->hqk', query_block, keys_all, preferred_element_type=...  44.7 us
    ppermute x36, starting transfers between devices, scatter_dp(): got = lax.ppermute(send, 'dp', [(i, i ^ 1 << bit) for i in range(n)])  42.4 us
    ppermute x9, waiting for transfers between devices, sum_all(): lax.ppermute(vector, axis, [(i, i ^ 1 << bit) for i in range(n)])  32.7 us
    reduce_sum x2, other arithmetic, backward_block(): jnp.sum(grad_scores.astype(jnp.float32) * distance[None], axis=(1, 2))  28.7 us
    dot_general x1, matrix products, shards(): jnp.einsum('le,fe->lf', grad_rows, w_down, preferred_element_type=jnp.flo...  24.9 us
    dot_general x2, matrix products, forward_block(): jnp.einsum('hqk,khd->qhd', weights_low, values_all, preferred_element_typ...  19.7 us
    unnamed x144, local copies, waits for them, and re-layouts  18.6 us
  transfers between devices with their start and end apart: 53, of which 23 were waited for; matrix products, arithmetic and copies ran while one was open for 54% of the time, Pallas kernels for 0%

profile of v1, /device:TPU:0, one launch (start us, length us, event | category | flops | bytes accessed | tf_op | source)
XLA Modules:
  0.0 603.2 jit_solution(9991141568819194426)
XLA Ops:
  101.1 69.3 %while.33 = (s32[]{:T(128)}, bf16[2,512,4,128]{3,2,1,0:T(4,128)(2,1)}, f32[2,4,512]{2,1,0:T(4,128)}, s32[2]{0:T(128)S(1)}, s32[1,4]{1,0:T(1,128)S(1)}, /*index=5...) while((s32[]{:T(128)}, ...), condition=%wide.region_11.13_spmd, body=%wide.region_6.12_spmd.sunk | while | flops 2090293248 | bytes 87024696 | solution.py:177
  107.6 8.1 %fusion.211 = (f32[4,512]{1,0:T(4,128)S(1)}, f32[4,512,1920]{2,1,0:T(8,128)}) fusion(f32[512,1920]{1,0:T(8,128)S(1)} %subtract_convert_fusion.4, f32[4]{0:T(128)S(1)} %get-tuple-element.826, pred[512,1920]{1,0:T(8,128)(4,1)S(1)} %pad_add_fusion.9, bf16[1920,4,128]{2,0,1:T(8,128)(2,1)S(1)} %copy-done.2, bf16[1024,4,128]{2,0,1:T(8,128)(2,1)S(1)} %copy-done.6, ...), kind=kOutput, calls=%fused_computation.4.clone.1 | convolution fusion | flops 1026291712 | bytes 23142916 | tf_op jit(solution)/shard_map/while/body/eval_jaxpr/qhd,khd->hqk/dot_general | solution.py:160
  115.7 8.5 %fusion.212 = f32[4,512]{1,0:T(4,128)S(1)} fusion(f32[4,512,1920]{2,1,0:T(8,128)} %get-tuple-element.766, f32[4,512]{1,0:T(4,128)S(1)} %get-tuple-element.767, f32[512,1920]{1,0:T(8,128)S(1)} %subtract_convert_fusion.4, f32[4]{0:T(128)S(1)} %get-tuple-element.826, pred[512,1920]{1,0:T(8,128)(4,1)S(1)} %pad_add_fusion.9), kind=kLoop, calls=%fused_computation.3.clone.1 | loop fusion | flops 23590912 | bytes 20660240 | tf_op jit(solution)/shard_map/while/body/eval_jaxpr/reduce_sum | solution.py:170
  124.8 9.9 %fusion.213 = bf16[1,512,4,128]{3,1,2,0:T(8,128)(2,1)S(1)} fusion(bf16[1920,4,128]{2,0,1:T(8,128)(2,1)S(1)} %get-tuple-element.827, f32[4,512,1920]{2,1,0:T(8,128)} %get-tuple-element.766, f32[4,512]{1,0:T(4,128)S(1)} %fusion.212, f32[4,512]{1,0:T(4,128)S(1)} %get-tuple-element.767, f32[512,1920]{1,0:T(8,128)S(1)} %subtract_convert_fusion.4, ...), kind=kOutput, calls=%fused_computation.11.clone.1 | convolution fusion | flops 1034420224 | bytes 23150608 | tf_op jit(solution)/shard_map/while/body/eval_jaxpr/hqk,khd->qhd/dot_general | solution.py:172
  142.1 8.1 %fusion.211 = (f32[4,512]{1,0:T(4,128)S(1)}, f32[4,512,1920]{2,1,0:T(8,128)}) fusion(f32[512,1920]{1,0:T(8,128)S(1)} %subtract_convert_fusion.4, f32[4]{0:T(128)S(1)} %get-tuple-element.826, pred[512,1920]{1,0:T(8,128)(4,1)S(1)} %pad_add_fusion.9, bf16[1920,4,128]{2,0,1:T(8,128)(2,1)S(1)} %copy-done.2, bf16[1024,4,128]{2,0,1:T(8,128)(2,1)S(1)} %copy-done.6, ...), kind=kOutput, calls=%fused_computation.4.clone.1 | convolution fusion | flops 1026291712 | bytes 23142916 | tf_op jit(solution)/shard_map/while/body/eval_jaxpr/qhd,khd->hqk/dot_general | solution.py:160
  150.2 8.5 %fusion.212 = f32[4,512]{1,0:T(4,128)S(1)} fusion(f32[4,512,1920]{2,1,0:T(8,128)} %get-tuple-element.766, f32[4,512]{1,0:T(4,128)S(1)} %get-tuple-element.767, f32[512,1920]{1,0:T(8,128)S(1)} %subtract_convert_fusion.4, f32[4]{0:T(128)S(1)} %get-tuple-element.826, pred[512,1920]{1,0:T(8,128)(4,1)S(1)} %pad_add_fusion.9), kind=kLoop, calls=%fused_computation.3.clone.1 | loop fusion | flops 23590912 | bytes 20660240 | tf_op jit(solution)/shard_map/while/body/eval_jaxpr/reduce_sum | solution.py:170
  159.3 9.9 %fusion.213 = bf16[1,512,4,128]{3,1,2,0:T(8,128)(2,1)S(1)} fusion(bf16[1920,4,128]{2,0,1:T(8,128)(2,1)S(1)} %get-tuple-element.827, f32[4,512,1920]{2,1,0:T(8,128)} %get-tuple-element.766, f32[4,512]{1,0:T(4,128)S(1)} %fusion.212, f32[4,512]{1,0:T(4,128)S(1)} %get-tuple-element.767, f32[512,1920]{1,0:T(8,128)S(1)} %subtract_convert_fusion.4, ...), kind=kOutput, calls=%fused_computation.11.clone.1 | convolution fusion | flops 1034420224 | bytes 23150608 | tf_op jit(solution)/shard_map/while/body/eval_jaxpr/hqk,khd->qhd/dot_general | solution.py:172
  200.5 24.9 %add_convert_fusion = (bf16[1024,2048]{1,0:T(8,128)(2,1)}, f32[1024,2048]{1,0:T(8,128)}) fusion(f32[1024,2048]{1,0:T(8,128)S(1)} %fusion.154, bf16[1024,1024]{0,1:T(8,128)(2,1)S(1)} %get-tuple-element.609, bf16[2048,1024]{1,0:T(8,128)(2,1)S(1)} %copy-done.74), kind=kOutput, calls=%fused_computation.73 | convolution fusion | flops 4445962240 | bytes 27262976 | tf_op jit(solution)/shard_map/le,fe->lf/dot_general | solution.py:194
  225.4 10.0 %multiply_convert_fusion.1 = bf16[1024,2048]{1,0:T(8,128)(2,1)} fusion(f32[1024,2048]{1,0:T(8,128)} %get-tuple-element.572, f32[1024,2048]{1,0:T(8,128)} %copy-done.20), kind=kLoop, calls=%fused_computation.74 | loop fusion | flops 6291456 | bytes 20971520 | tf_op jit(solution)/shard_map/convert_element_type | solution.py:185
  235.4 7.5 %convolution_convert_fusion = bf16[1024,2048]{1,0:T(8,128)(2,1)S(1)} fusion(bf16[1024,1024]{0,1:T(8,128)(2,1)} %copy-done.38, bf16[1024,2048]{1,0:T(8,128)(2,1)} %multiply_convert_fusion.1), kind=kOutput, calls=%fused_computation.111 | convolution fusion | flops 4297064448 | bytes 10485760 | tf_op jit(solution)/shard_map/lf,le->ef/dot_general | solution.py:197
  275.1 23.9 %collective-permute-done.37 = bf16[2,2,2,64,2048]{4,3,2,0,1:T(8,128)(2,1)} collective-permute-done((bf16[2,2,2,64,2048]{4,3,2,0,1:T(8,128)(2,1)}, bf16[2,2,2,64,2048]{4,3,2,0,1:T(8,128)(2,1)}, u32[]{:S(2)}, u32[]{:S(2)}) %collective-permute-start.37) | collective-permute-done | bytes 2097184 | tf_op jit(solution)/shard_map/ppermute | solution.py:72
  311.3 126.7 %while.34 = (s32[]{:T(128)}, f32[1920,4,128]{0,2,1:T(8,128)}, f32[1920,4,128]{0,2,1:T(8,128)}, f32[4]{0:T(128)S(1)}, bf16[2,512,4,128]{3,2,1,0:T(4,128)(2,1)}, /...) while((s32[]{:T(128)}, f32[1920,4,128]{0,2,1:T(8,128)}, ...), condition=%wide.region_21.23_spmd.clone, body=%wide.region_16.22_spmd.clone.sunk | while | flops 5099640832 | bytes 235176032 | solution.py:251
  315.8 8.9 %fusion.223 = f32[4,512,1920]{2,1,0:T(8,128)} fusion(bf16[1920,4,128]{2,0,1:T(8,128)(2,1)S(1)} %get-tuple-element.881, bf16[1024,4,128]{0,2,1:T(8,128)(2,1)} %get-tuple-element.880, s32[]{:T(128)S(6)} %select_n.200), kind=kOutput, calls=%fused_computation.48.clone.1 | convolution fusion | flops 1006632960 | bytes 18219012 | tf_op jit(solution)/shard_map/while/body/eval_jaxpr/qhd,khd->hqk/dot_general | solution.py:223
  326.0 14.2 %multiply_reduce_fusion.7 = (f32[4,512]{1,0:T(4,128)S(1)}, f32[4,512,1920]{2,1,0:T(8,128)}) fusion(f32[4,512,1920]{2,1,0:T(8,128)} %fusion.223, f32[4,512]{1,0:T(4,128)S(1)} %dynamic-slice_bitcast_fusion.29, f32[512,1920]{1,0:T(8,128)S(1)} %subtract_convert_fusion.5, f32[4]{0:T(128)} %copy-done.56, bf16[1920,4,128]{2,0,1:T(8,128)(2,1)} %get-tuple-element.877, ...), kind=kOutput, calls=%fused_computation.33.clone.1 | convolution fusion | flops 1034156032 | bytes 38879252 | tf_op jit(solution)/shard_map/while/body/eval_jaxpr/qhd,khd->hqk/dot_general | solution.py:160
  340.2 14.4 %multiply_reduce_fusion.8 = (f32[4]{0:T(128)S(1)}, bf16[4,512,1920]{2,1,0:T(8,128)(2,1)}) fusion(f32[512,1920]{1,0:T(8,128)S(1)} %subtract_convert_fusion.5, f32[4,512,1920]{2,1,0:T(8,128)} %get-tuple-element.785, f32[4,512,1920]{2,1,0:T(8,128)} %fusion.223, f32[4,512]{1,0:T(4,128)S(1)} %get-tuple-element.786), kind=kLoop, calls=%fused_computation.31.clone.1 | loop fusion | flops 23592956 | bytes 43261968 | tf_op jit(solution)/shard_map/while/body/eval_jaxpr/reduce_sum | solution.py:228
  354.6 6.8 %bitcast_add_fusion.4 = f32[1920,4,128]{0,2,1:T(8,128)} fusion(f32[1920,4,128]{0,2,1:T(8,128)} %get-tuple-element.850, bf16[4,512,1920]{2,1,0:T(8,128)(2,1)} %get-tuple-element.787, pred[]{:T(512)S(6)} %compare.4, bf16[1024,4,128]{2,0,1:T(8,128)(2,1)S(1)} %copy-done.8, s32[]{:T(128)S(6)} %select_n.200), kind=kOutput, calls=%fused_computation.38.clone.1 | convolution fusion | flops 1009582080 | bytes 16252933 | tf_op jit(solution)/shard_map/while/body/eval_jaxpr/hqk,qhd->khd/dot_general | solution.py:237
  377.4 8.8 %fusion.223 = f32[4,512,1920]{2,1,0:T(8,128)} fusion(bf16[1920,4,128]{2,0,1:T(8,128)(2,1)S(1)} %get-tuple-element.881, bf16[1024,4,128]{0,2,1:T(8,128)(2,1)} %get-tuple-element.880, s32[]{:T(128)S(6)} %select_n.200), kind=kOutput, calls=%fused_computation.48.clone.1 | convolution fusion | flops 1006632960 | bytes 18219012 | tf_op jit(solution)/shard_map/while/body/eval_jaxpr/qhd,khd->hqk/dot_general | solution.py:223
  387.5 14.2 %multiply_reduce_fusion.7 = (f32[4,512]{1,0:T(4,128)S(1)}, f32[4,512,1920]{2,1,0:T(8,128)}) fusion(f32[4,512,1920]{2,1,0:T(8,128)} %fusion.223, f32[4,512]{1,0:T(4,128)S(1)} %dynamic-slice_bitcast_fusion.29, f32[512,1920]{1,0:T(8,128)S(1)} %subtract_convert_fusion.5, f32[4]{0:T(128)} %copy-done.56, bf16[1920,4,128]{2,0,1:T(8,128)(2,1)} %get-tuple-element.877, ...), kind=kOutput, calls=%fused_computation.33.clone.1 | convolution fusion | flops 1034156032 | bytes 38879252 | tf_op jit(solution)/shard_map/while/body/eval_jaxpr/qhd,khd->hqk/dot_general | solution.py:160
  401.7 14.4 %multiply_reduce_fusion.8 = (f32[4]{0:T(128)S(1)}, bf16[4,512,1920]{2,1,0:T(8,128)(2,1)}) fusion(f32[512,1920]{1,0:T(8,128)S(1)} %subtract_convert_fusion.5, f32[4,512,1920]{2,1,0:T(8,128)} %get-tuple-element.785, f32[4,512,1920]{2,1,0:T(8,128)} %fusion.223, f32[4,512]{1,0:T(4,128)S(1)} %get-tuple-element.786), kind=kLoop, calls=%fused_computation.31.clone.1 | loop fusion | flops 23592956 | bytes 43261968 | tf_op jit(solution)/shard_map/while/body/eval_jaxpr/reduce_sum | solution.py:228
  416.1 8.0 %bitcast_add_fusion.4 = f32[1920,4,128]{0,2,1:T(8,128)} fusion(f32[1920,4,128]{0,2,1:T(8,128)} %get-tuple-element.850, bf16[4,512,1920]{2,1,0:T(8,128)(2,1)} %get-tuple-element.787, pred[]{:T(512)S(6)} %compare.4, bf16[1024,4,128]{2,0,1:T(8,128)(2,1)S(1)} %copy-done.8, s32[]{:T(128)S(6)} %select_n.200), kind=kOutput, calls=%fused_computation.38.clone.1 | convolution fusion | flops 1009582080 | bytes 16252933 | tf_op jit(solution)/shard_map/while/body/eval_jaxpr/hqk,qhd->khd/dot_general | solution.py:237
  486.3 7.1 %collective-permute-done.17 = bf16[2,2,2,64,512]{4,3,2,0,1:T(8,128)(2,1)S(1)} collective-permute-done((bf16[2,2,2,64,512]{4,3,2,0,1:T(8,128)(2,1)S(1)}, bf16[2,2,2,64,512]{4,3,2,0,1:T(8,128)(2,1)S(1)}, u32[]{:S(2)}, u32[]{:S(2)}) %collective-permute-start.17) | collective-permute-done | bytes 524320 | tf_op jit(solution)/shard_map/ppermute | solution.py:72
  507.1 10.0 %collective-permute-done.18 = bf16[2,2,64,512]{3,2,1,0:T(8,128)(2,1)S(1)} collective-permute-done((bf16[2,2,64,512]{3,2,1,0:T(8,128)(2,1)S(1)}, bf16[2,2,64,512]{3,2,1,0:T(8,128)(2,1)S(1)}, u32[]{:S(2)}, u32[]{:S(2)}) %collective-permute-start.18) | collective-permute-done | bytes 262176 | tf_op jit(solution)/shard_map/ppermute | solution.py:72
  559.4 20.6 %collective-permute-done.11 = f32[2,1024]{1,0:T(2,128)S(1)} collective-permute-done((f32[2,1024]{1,0:T(2,128)S(1)}, f32[2,1024]{1,0:T(2,128)S(1)}, u32[]{:S(2)}, u32[]{:S(2)}) %collective-permute-start.11) | collective-permute-done | bytes 8224 | tf_op jit(solution)/shard_map/ppermute | solution.py:83
  593.8 8.1 %collective-permute-done.36 = bf16[64,2048]{1,0:T(8,128)(2,1)S(1)} collective-permute-done((bf16[64,2048]{1,0:T(8,128)(2,1)S(1)}, bf16[64,2048]{1,0:T(8,128)(2,1)S(1)}, u32[]{:S(2)}, u32[]{:S(2)}) %collective-permute-start.36) | collective-permute-done | bytes 262176 | tf_op jit(solution)/shard_map/ppermute | solution.py:72
  (549 shorter events, 335.4 us)
Async XLA Ops:
  11.9 46.9 %collective-permute-start.49 = (bf16[2,2,2,64,512]{4,3,1,2,0:T(8,128)(2,1)}, bf16[2,2,2,64,512]{4,3,1,2,0:T(8,128)(2,1)}, u32[]{:S(2)}, u32[]{:S(2)}) collective-permute-start(bf16[2,2,2,64,512]{4,3,1,2,0:T(8,128)(2,1)} %bitcast.412), channel_id=1, source_target_pairs={{0,8},{2,10},{4,12},{6,14},{8,0},{10,2},{12,4},{14,6},{16,24},{18,... | collective-permute-start | bytes 1572872 | tf_op jit(solution)/shard_map/ppermute | solution.py:72
  20.3 42.5 %collective-permute-start.45 = (bf16[2,2,2,64,512]{4,3,2,0,1:T(8,128)(2,1)}, bf16[2,2,2,64,512]{4,3,2,0,1:T(8,128)(2,1)}, u32[]{:S(2)}, u32[]{:S(2)}) collective-permute-start(bf16[2,2,2,64,512]{4,3,2,0,1:T(8,128)(2,1)} %bitcast.413), channel_id=1, source_target_pairs={{0,4},{2,6},{4,0},{6,2},{8,12},{10,14},{12,8},{14,10},{16,20},{18,... | collective-permute-start | bytes 1572872 | tf_op jit(solution)/shard_map/ppermute | solution.py:72
  27.3 37.4 %collective-permute-start.41 = (bf16[2,2,2,64,512]{4,3,0,1,2:T(8,128)(2,1)}, bf16[2,2,2,64,512]{4,3,0,1,2:T(8,128)(2,1)}, u32[]{:S(2)}, u32[]{:S(2)}) collective-permute-start(bf16[2,2,2,64,512]{4,3,0,1,2:T(8,128)(2,1)} %bitcast.414), channel_id=1, source_target_pairs={{0,2},{2,0},{4,6},{6,4},{8,10},{10,8},{12,14},{14,12},{16,18},{18,... | collective-permute-start | bytes 1572872 | tf_op jit(solution)/shard_map/ppermute | solution.py:72
  43.4 35.1 %collective-permute-start = (bf16[512,1024]{0,1:T(8,128)(2,1)}, bf16[512,1024]{0,1:T(8,128)(2,1)}, u32[]{:S(2)}, u32[]{:S(2)}) collective-permute-start(bf16[512,1024]{0,1:T(8,128)(2,1)} %get-tuple-element.608), channel_id=1, source_target_pairs={{0,1},{1,0},{2,3},{3,2},{4,5},{5,4},{6,7},{7,6},{8,9},{9,8},{10,11... | collective-permute-start | bytes 3145736 | tf_op jit(solution)/shard_map/ppermute | solution.py:41
  45.8 145.7 %collective-permute-start.4 = (bf16[512,1024]{0,1:T(8,128)(2,1)}, bf16[512,1024]{0,1:T(8,128)(2,1)}, u32[]{:S(2)}, u32[]{:S(2)}) collective-permute-start(bf16[512,1024]{0,1:T(8,128)(2,1)} %bitcast.457), channel_id=1, source_target_pairs={{0,1},{1,0},{2,3},{3,2},{4,5},{5,4},{6,7},{7,6},{8,9},{9,8},{10,11... | collective-permute-start | bytes 3145736 | tf_op jit(solution)/shard_map/ppermute | solution.py:41
  60.2 14.8 %collective-permute-start.50 = (bf16[2,2,64,512]{3,2,0,1:T(8,128)(2,1)S(1)}, bf16[2,2,64,512]{3,2,0,1:T(8,128)(2,1)S(1)}, u32[]{:S(2)}, u32[]{:S(2)}) collective-permute-start(bf16[2,2,64,512]{3,2,0,1:T(8,128)(2,1)S(1)} %dynamic-slice_bitcast_fusion.5), channel_id=1, source_target_pairs={{0,16},{2,18},{4,20},{6,22},{8,24},{10,26},{12,28},{14,30},{16,0},... | collective-permute-start | bytes 786440 | tf_op jit(solution)/shard_map/ppermute | solution.py:72
  64.2 13.5 %collective-permute-start.46 = (bf16[2,2,64,512]{3,2,1,0:T(8,128)(2,1)S(1)}, bf16[2,2,64,512]{3,2,1,0:T(8,128)(2,1)S(1)}, u32[]{:S(2)}, u32[]{:S(2)}) collective-permute-start(bf16[2,2,64,512]{3,2,1,0:T(8,128)(2,1)S(1)} %dynamic-slice_bitcast_fusion.6), channel_id=1, source_target_pairs={{0,8},{2,10},{4,12},{6,14},{8,0},{10,2},{12,4},{14,6},{16,24},{18,... | collective-permute-start | bytes 786440 | tf_op jit(solution)/shard_map/ppermute | solution.py:72
  67.8 106.0 %collective-permute-start.42 = (bf16[2,2,64,512]{3,2,0,1:T(8,128)(2,1)}, bf16[2,2,64,512]{3,2,0,1:T(8,128)(2,1)}, u32[]{:S(2)}, u32[]{:S(2)}) collective-permute-start(bf16[2,2,64,512]{3,2,0,1:T(8,128)(2,1)} %dynamic-slice_bitcast_fusion.7), channel_id=1, source_target_pairs={{0,4},{2,6},{4,0},{6,2},{8,12},{10,14},{12,8},{14,10},{16,20},{18,... | collective-permute-start | bytes 786440 | tf_op jit(solution)/shard_map/ppermute | solution.py:72
  75.8 100.7 %collective-permute-start.51 = (bf16[2,64,512]{2,1,0:T(8,128)(2,1)}, bf16[2,64,512]{2,1,0:T(8,128)(2,1)}, u32[]{:S(2)}, u32[]{:S(2)}) collective-permute-start(bf16[2,64,512]{2,1,0:T(8,128)(2,1)} %dynamic-slice_bitcast_fusion.14), channel_id=1, source_target_pairs={{0,2},{2,0},{4,6},{6,4},{8,10},{10,8},{12,14},{14,12},{16,18},{18,... | collective-permute-start | bytes 393224 | tf_op jit(solution)/shard_map/ppermute | solution.py:72
  251.1 47.9 %collective-permute-start.37 = (bf16[2,2,2,64,2048]{4,3,2,0,1:T(8,128)(2,1)}, bf16[2,2,2,64,2048]{4,3,2,0,1:T(8,128)(2,1)}, u32[]{:S(2)}, u32[]{:S(2)}) collective-permute-start(bf16[2,2,2,64,2048]{4,3,2,0,1:T(8,128)(2,1)} %bitcast.410), channel_id=1, source_target_pairs={{0,4},{2,6},{4,0},{6,2},{8,12},{10,14},{12,8},{14,10},{16,20},{18,... | collective-permute-start | bytes 6291464 | tf_op jit(solution)/shard_map/ppermute | solution.py:72
  269.1 35.4 %collective-permute-start.6 = (bf16[512,1024]{0,1:T(8,128)(2,1)}, bf16[512,1024]{0,1:T(8,128)(2,1)}, u32[]{:S(2)}, u32[]{:S(2)}) collective-permute-start(bf16[512,1024]{0,1:T(8,128)(2,1)} %fusion.78), channel_id=1, source_target_pairs={{0,1},{1,0},{2,3},{3,2},{4,5},{5,4},{6,7},{7,6},{8,9},{9,8},{10,11... | collective-permute-start | bytes 3145736 | tf_op jit(solution)/shard_map/ppermute | solution.py:41
  272.4 175.7 %collective-permute-start.33 = (bf16[2,2,2,64,2048]{4,3,0,1,2:T(8,128)(2,1)}, bf16[2,2,2,64,2048]{4,3,0,1,2:T(8,128)(2,1)}, u32[]{:S(2)}, u32[]{:S(2)}) collective-permute-start(bf16[2,2,2,64,2048]{4,3,0,1,2:T(8,128)(2,1)} %bitcast.411), channel_id=1, source_target_pairs={{0,2},{2,0},{4,6},{6,4},{8,10},{10,8},{12,14},{14,12},{16,18},{18,... | collective-permute-start | bytes 6291464 | tf_op jit(solution)/shard_map/ppermute | solution.py:72
  304.5 241.5 %collective-permute-start.38 = (bf16[2,2,64,2048]{3,2,1,0:T(8,128)(2,1)}, bf16[2,2,64,2048]{3,2,1,0:T(8,128)(2,1)}, u32[]{:S(2)}, u32[]{:S(2)}) collective-permute-start(bf16[2,2,64,2048]{3,2,1,0:T(8,128)(2,1)} %dynamic-slice_bitcast_fusion.1), channel_id=1, source_target_pairs={{0,8},{2,10},{4,12},{6,14},{8,0},{10,2},{12,4},{14,6},{16,24},{18,... | collective-permute-start | bytes 3145736 | tf_op jit(solution)/shard_map/ppermute | solution.py:72
  450.7 100.3 %collective-permute-start.34 = (bf16[2,2,64,2048]{3,2,0,1:T(8,128)(2,1)S(1)}, bf16[2,2,64,2048]{3,2,0,1:T(8,128)(2,1)S(1)}, u32[]{:S(2)}, u32[]{:S(2)}) collective-permute-start(bf16[2,2,64,2048]{3,2,0,1:T(8,128)(2,1)S(1)} %dynamic-slice_bitcast_fusion.2), channel_id=1, source_target_pairs={{0,4},{2,6},{4,0},{6,2},{8,12},{10,14},{12,8},{14,10},{16,20},{18,... | collective-permute-start | bytes 3145736 | tf_op jit(solution)/shard_map/ppermute | solution.py:72
  451.4 32.8 %collective-permute-start.29 = (bf16[2,2,2,64,512]{4,3,1,2,0:T(8,128)(2,1)S(1)}, bf16[2,2,2,64,512]{4,3,1,2,0:T(8,128)(2,1)S(1)}, u32[]{:S(2)}, u32[]{:S(2)}) collective-permute-start(bf16[2,2,2,64,512]{4,3,1,2,0:T(8,128)(2,1)S(1)} %bitcast.477), channel_id=1, source_target_pairs={{0,8},{2,10},{4,12},{6,14},{8,0},{10,2},{12,4},{14,6},{16,24},{18,... | collective-permute-start | bytes 1572872 | tf_op jit(solution)/shard_map/ppermute | solution.py:72
  453.4 14.3 %collective-permute-start.25 = (f32[4]{0:T(128)S(1)}, f32[4]{0:T(128)S(1)}, u32[]{:S(2)}, u32[]{:S(2)}) collective-permute-start(f32[4]{0:T(128)S(1)} %get-tuple-element.351), channel_id=1, source_target_pairs={{0,2},{2,0},{4,6},{6,4},{8,10},{10,8},{12,14},{14,12},{16,18},{18,... | collective-permute-start | bytes 56 | tf_op jit(solution)/shard_map/ppermute | solution.py:83
  456.2 29.8 %collective-permute-start.13 = (bf16[2,2,2,64,512]{4,3,0,1,2:T(8,128)(2,1)S(1)}, bf16[2,2,2,64,512]{4,3,0,1,2:T(8,128)(2,1)S(1)}, u32[]{:S(2)}, u32[]{:S(2)}) collective-permute-start(bf16[2,2,2,64,512]{4,3,0,1,2:T(8,128)(2,1)S(1)} %bitcast.478), channel_id=1, source_target_pairs={{0,2},{2,0},{4,6},{6,4},{8,10},{10,8},{12,14},{14,12},{16,18},{18,... | collective-permute-start | bytes 1572872 | tf_op jit(solution)/shard_map/ppermute | solution.py:72
  486.0 58.2 %collective-permute-start.7 = (bf16[512,1024]{0,1:T(8,128)(2,1)S(1)}, bf16[512,1024]{0,1:T(8,128)(2,1)S(1)}, u32[]{:S(2)}, u32[]{:S(2)}) collective-permute-start(bf16[512,1024]{0,1:T(8,128)(2,1)S(1)} %dynamic-slice_convert_fusion), channel_id=1, source_target_pairs={{0,1},{1,0},{2,3},{3,2},{4,5},{5,4},{6,7},{7,6},{8,9},{9,8},{10,11... | collective-permute-start | bytes 3145736 | tf_op jit(solution)/shard_map/ppermute | solution.py:41
  504.3 12.7 %collective-permute-start.18 = (bf16[2,2,64,512]{3,2,1,0:T(8,128)(2,1)S(1)}, bf16[2,2,64,512]{3,2,1,0:T(8,128)(2,1)S(1)}, u32[]{:S(2)}, u32[]{:S(2)}) collective-permute-start(bf16[2,2,64,512]{3,2,1,0:T(8,128)(2,1)S(1)} %dynamic-slice_bitcast_fusion.12), channel_id=1, source_target_pairs={{0,8},{2,10},{4,12},{6,14},{8,0},{10,2},{12,4},{14,6},{16,24},{18,... | collective-permute-start | bytes 786440 | tf_op jit(solution)/shard_map/ppermute | solution.py:72
  528.2 15.3 %collective-permute-start.32 = (bf16[64,512]{1,0:T(8,128)(2,1)S(1)}, bf16[64,512]{1,0:T(8,128)(2,1)S(1)}, u32[]{:S(2)}, u32[]{:S(2)}) collective-permute-start(bf16[64,512]{1,0:T(8,128)(2,1)S(1)} %dynamic-slice_bitcast_fusion.24), channel_id=1, source_target_pairs={{0,4},{2,6},{4,0},{6,2},{8,12},{10,14},{12,8},{14,10},{16,20},{18,... | collective-permute-start | bytes 196616 | tf_op jit(solution)/shard_map/ppermute | solution.py:72
  548.7 36.4 %collective-permute-start.39 = (bf16[2,64,2048]{2,1,0:T(8,128)(2,1)}, bf16[2,64,2048]{2,1,0:T(8,128)(2,1)}, u32[]{:S(2)}, u32[]{:S(2)}) collective-permute-start(bf16[2,64,2048]{2,1,0:T(8,128)(2,1)} %dynamic-slice_bitcast_fusion.3), channel_id=1, source_target_pairs={{0,16},{2,18},{4,20},{6,22},{8,24},{10,26},{12,28},{14,30},{16,0},... | collective-permute-start | bytes 1572872 | tf_op jit(solution)/shard_map/ppermute | solution.py:72
  554.8 33.0 %collective-permute-start.35 = (bf16[2,64,2048]{2,1,0:T(8,128)(2,1)}, bf16[2,64,2048]{2,1,0:T(8,128)(2,1)}, u32[]{:S(2)}, u32[]{:S(2)}) collective-permute-start(bf16[2,64,2048]{2,1,0:T(8,128)(2,1)} %dynamic-slice_bitcast_fusion.4), channel_id=1, source_target_pairs={{0,8},{2,10},{4,12},{6,14},{8,0},{10,2},{12,4},{14,6},{16,24},{18,... | collective-permute-start | bytes 1572872 | tf_op jit(solution)/shard_map/ppermute | solution.py:72
  557.3 22.6 %collective-permute-start.11 = (f32[2,1024]{1,0:T(2,128)S(1)}, f32[2,1024]{1,0:T(2,128)S(1)}, u32[]{:S(2)}, u32[]{:S(2)}) collective-permute-start(f32[2,1024]{1,0:T(2,128)S(1)} %add.467), channel_id=1, source_target_pairs={{0,8},{2,10},{4,12},{6,14},{8,0},{10,2},{12,4},{14,6},{16,24},{18,... | collective-permute-start | bytes 24584 | tf_op jit(solution)/shard_map/ppermute | solution.py:83
  589.2 12.7 %collective-permute-start.36 = (bf16[64,2048]{1,0:T(8,128)(2,1)S(1)}, bf16[64,2048]{1,0:T(8,128)(2,1)S(1)}, u32[]{:S(2)}, u32[]{:S(2)}) collective-permute-start(bf16[64,2048]{1,0:T(8,128)(2,1)S(1)} %dynamic-slice_bitcast_fusion.9), channel_id=1, source_target_pairs={{0,16},{2,18},{4,20},{6,22},{8,24},{10,26},{12,28},{14,30},{16,0},... | collective-permute-start | bytes 786440 | tf_op jit(solution)/shard_map/ppermute | solution.py:72
  (128 other events, 1076.7 us)
